TPU v7x, 32 devices: a whole 2x2x4 slice. The times are simulated.
32 devices in a mesh: layer: 4 (over z), row: 8 (over y, x, core).
Axes of the slice: x: 2, y: 2, z: 4, core: 2. Of those that a mesh axis runs over, the one named last changes fastest.
Arguments:
- rhs_sub: float32 [4, 3, 4096, 256], P('layer', None, 'row'), may hold values from -6 to 6
- rhs_root: float32 [2048, 256], P('row'), may hold values from -6 to 6
- lower_inv: float32 [4, 3, 4096, 4096], P('layer', None, 'row'), may hold values from -0.09375 to 0.09375
- upper_inv: float32 [4, 3, 4096, 4096], P('layer', None, 'row'), may hold values from -0.09375 to 0.09375
- coupling_low: float32 [4, 3, 2048, 4096], P('layer', None, None, 'row'), may hold values from -0.0390625 to 0.0390625
- coupling_up: float32 [4, 3, 4096, 2048], P('layer', None, 'row'), may hold values from -0.1875 to 0.1875
- tile_mask: int32 [4, 3, 16, 32], P('layer', None, None, 'row'), may hold values 0 or 1
- root_inv: float32 [2048, 2048], P('row'), may hold values from -0.125 to 0.125
Outputs:
- sol_sub: float32 [4, 3, 4096, 256], P('layer', None, 'row')
- sol_root: float32 [2048, 256], P('row')
All inputs are finite; a program needn't handle non-finite values. No bound on the sum of `tile_mask` on one device may be relied on, other than what follows from the above.
Results may differ from a plain program's by a relative error of at most 0.0001.
Values sent between devices are 32-bit elements; how exact they have to be, the bound alone decides.
A program may use at most 192 MiB of HBM per device.

v0:
```python
import jax
import jax.numpy as jnp
from jax import lax
from jax.sharding import PartitionSpec as P

TILE = 128


def masked_tiles(coupling, pattern, tile, flipped):
    blocks, height, breadth = coupling.shape
    shaped = coupling.reshape(blocks, height // tile, tile, breadth // tile, tile)
    if flipped:
        pattern = jnp.transpose(pattern, (0, 2, 1))
    weights = pattern.astype(jnp.float32)[:, :, None, :, None]
    return (shaped * weights).reshape(blocks, height, breadth)


def fold_stacked(matrices, piece):
    return jnp.einsum("kij,kjr->kir", matrices, piece, precision=lax.Precision.HIGHEST)


def body(rhs_sub, rhs_root, lower_inv, upper_inv, coupling_low, coupling_up, tile_mask, root_inv):
    highest = lax.Precision.HIGHEST
    lower = lower_inv[0]
    upper = upper_inv[0]
    vectors = rhs_sub[0]
    interim = fold_stacked(lower, lax.all_gather(vectors, "row", axis=1, tiled=True))
    lower_coupling = masked_tiles(coupling_low[0], tile_mask[0], TILE, False)
    local_part = lax.psum_scatter(
        jnp.einsum("kas,ksr->ar", lower_coupling, interim, precision=highest),
        "row",
        scatter_dimension=0,
        tiled=True,
    )
    layer_total = lax.psum(local_part, "layer")
    reduced = rhs_root - layer_total
    columns = root_inv
    sol_root = jnp.dot(
        columns,
        lax.all_gather(reduced, "row", axis=0, tiled=True),
        precision=highest,
        preferred_element_type=jnp.float32,
    )
    upper_coupling = masked_tiles(coupling_up[0], tile_mask[0], TILE, True)
    columns = upper_coupling
    coupled = jnp.einsum(
        "ksa,ar->ksr",
        columns,
        lax.all_gather(sol_root, "row", axis=0, tiled=True),
        precision=highest,
    )
    residue = interim - coupled
    solved = fold_stacked(upper, lax.all_gather(residue, "row", axis=1, tiled=True))
    return (solved[None], sol_root)


def solution(mesh):
    return jax.shard_map(
        body,
        mesh=mesh,
        in_specs=(
            P("layer", None, "row", None),
            P("row", None),
            P("layer", None, "row", None),
            P("layer", None, "row", None),
            P("layer", None, None, "row"),
            P("layer", None, "row", None),
            P("layer", None, None, "row"),
            P("row", None),
        ),
        out_specs=(P("layer", None, "row", None), P("row", None)),
        check_vma=False,
    )
```

profile of v0, /device:TPU:0, one launch (start us, length us, event | category | flops | bytes accessed | tf_op | source)
XLA Modules:
  0.0 413.1 jit_solution(14953249950018203819)
XLA Ops:
  7.2 0.0 all-gather.12.cloned.1.call-start
  7.2 0.7 all-gather.12.cloned.1.call-update
  7.9 0.0 reduce-scatter.2.cloned.1.call-start
  8.0 0.7 convert_bitcast_fusion
  8.7 0.1 copy.10
  8.8 6.3 %mul.25 = f32[3,16,128,4,128]{4,3,2,1,0:T(4,128)} broadcast(f32[3,16,4]{2,1,0:T(8,128)S(1)} %copy.10), dimensions={0,1,3} | broadcast | bytes 12583680 | tf_op jit(solution)/shard_map/mul | solution.py:15
  15.0 15.4 %mul.26 = f32[3,2048,512]{2,1,0:T(8,128)} reshape(f32[3,16,128,4,128]{4,3,2,1,0:T(4,128)} %mul.25) | data formatting | bytes 25165824 | tf_op jit(solution)/shard_map/mul | solution.py:15
  30.4 54.4 %all-gather.12.cloned.1.call-done = f32[1,3,4096,256]{3,2,1,0:T(8,128)} async-done(((f32[1,3,512,256]{3,2,1,0:T(8,128)}), f32[1,3,4096,256]{3,2,1,0:T(8,128)}) %all-gather.12.cloned.1.call-update) | async-done | bytes 12582928 | tf_op jit(solution)/shard_map/all_gather | solution.py:27
  84.8 26.0 %fusion.2 = f32[3,512,256]{2,1,0:T(8,128)S(1)} fusion(f32[1,3,512,4096]{3,2,1,0:T(8,128)} %param.10, f32[1,3,4096,256]{3,2,1,0:T(8,128)} %all-gather.12.cloned.1.call-done), kind=kOutput, calls=%fused_computation.2 | convolution fusion | flops 19327352832 | bytes 39321600 | tf_op jit(solution)/shard_map/kij,kjr->kir/dot_general | solution.py:19
  110.8 1.1 copy-done.3
  112.0 13.9 %fusion.7 = f32[2048,256]{1,0:T(8,128)} fusion(f32[3,512,256]{2,1,0:T(8,128)S(1)} %fusion.2, f32[3,2048,512]{2,1,0:T(8,128)S(1)} %copy-done.2, f32[1,3,2048,512]{3,2,1,0:T(8,128)} %param.12), kind=kOutput, calls=%fused_computation.9 | convolution fusion | flops 9666822144 | bytes 28835840 | tf_op jit(solution)/shard_map/kas,ksr->ar/dot_general | solution.py:30
  125.9 0.0 reduce-scatter.2.cloned.1.call-update
  125.9 0.0 all-reduce.2.cloned.1.call-start
  126.0 41.3 %reduce-scatter.2.cloned.1.call-done = f32[256,256]{1,0:T(8,128)} async-done(((f32[2048,256]{1,0:T(8,128)}), f32[256,256]{1,0:T(8,128)}) %reduce-scatter.2.cloned.1.call-update) | async-done | bytes 262160 | tf_op jit(solution)/shard_map/reduce_scatter | solution.py:29
  167.3 0.0 all-reduce.2.cloned.1.call-update
  167.3 0.0 all-gather.6.cloned.1.call-start
  167.4 37.7 %all-reduce.2.cloned.1.call-done = f32[256,256]{1,0:T(8,128)} async-done(((f32[256,256]{1,0:T(8,128)}), f32[256,256]{1,0:T(8,128)}) %all-reduce.2.cloned.1.call-update) | async-done | bytes 262160 | tf_op jit(solution)/shard_map/psum | solution.py:35
  205.1 1.7 sub.6
  206.8 0.0 all-gather.6.cloned.1.call-update
  206.8 0.2 all-gather.8.cloned.1.call-start
  207.0 28.0 %all-gather.6.cloned.1.call-done = f32[2048,256]{1,0:T(8,128)} async-done(((f32[256,256]{1,0:T(8,128)}), f32[2048,256]{1,0:T(8,128)}) %all-gather.6.cloned.1.call-update) | async-done | bytes 2097168 | tf_op jit(solution)/shard_map/all_gather | solution.py:40
  235.1 5.8 %convolution_bitcast_fusion = f32[256,256]{0,1:T(8,128)} fusion(f32[2048,256]{1,0:T(8,128)} %all-gather.6.cloned.1.call-done, f32[256,2048]{1,0:T(8,128)S(1)} %copy-done), kind=kOutput, calls=%fused_computation.13 | convolution fusion | flops 1610612736 | bytes 4456448 | tf_op jit(solution)/shard_map/dot_general | solution.py:38
  240.8 0.0 all-gather.8.cloned.1.call-update
  240.9 0.0 all-gather.10.cloned.1.call-start
  240.9 5.4 %mul.22 = f32[3,4,128,16,128]{4,3,2,1,0:T(8,128)} broadcast(f32[3,4,16]{2,1,0:T(4,128)S(1)} %get-tuple-element.4), dimensions={0,1,3} | broadcast | bytes 12583680 | tf_op jit(solution)/shard_map/mul | solution.py:15
  246.3 13.8 %mul.23 = f32[3,512,2048]{2,1,0:T(8,128)} reshape(f32[3,4,128,16,128]{4,3,2,1,0:T(8,128)} %mul.22) | data formatting | bytes 25165824 | tf_op jit(solution)/shard_map/mul | solution.py:15
  260.1 9.1 %all-gather.8.cloned.1.call-done = f32[2048,256]{0,1:T(8,128)} async-done(((f32[256,256]{0,1:T(8,128)}), f32[2048,256]{0,1:T(8,128)}) %all-gather.8.cloned.1.call-update) | async-done | bytes 2097168 | tf_op jit(solution)/shard_map/all_gather | solution.py:49
  269.2 16.3 %fusion.12 = f32[3,512,256]{2,1,0:T(8,128)} fusion(f32[3,512,256]{2,1,0:T(8,128)S(1)} %copy-done.4, f32[2048,256]{0,1:T(8,128)} %all-gather.8.cloned.1.call-done, f32[3,512,2048]{2,1,0:T(8,128)} %mul.23, f32[1,3,512,2048]{3,2,1,0:T(8,128)} %param.13), kind=kOutput, calls=%fused_computation.12 | convolution fusion | flops 9667215360 | bytes 30408704 | tf_op jit(solution)/shard_map/ksa,ar->ksr/dot_general | solution.py:46
  285.5 0.8 copy.13
  286.4 71.4 %all-gather.10.cloned.1.call-done = f32[3,4096,256]{2,1,0:T(8,128)} async-done(((f32[3,512,256]{2,1,0:T(8,128)}), f32[3,4096,256]{2,1,0:T(8,128)}) %all-gather.10.cloned.1.call-update) | async-done | bytes 12582928 | tf_op jit(solution)/shard_map/all_gather | solution.py:53
  357.8 45.5 %fusion.9 = f32[1,3,512,256]{2,3,1,0:T(8,128)} fusion(f32[3,4096,256]{2,1,0:T(8,128)} %all-gather.10.cloned.1.call-done, f32[1,3,512,4096]{3,2,1,0:T(8,128)} %param.11), kind=kOutput, calls=%fused_computation.11 | convolution fusion | flops 19327352832 | bytes 39321600 | tf_op jit(solution)/shard_map/kij,kjr->kir/dot_general | solution.py:19
  403.3 3.0 copy.12
  (14 shorter events, 0.1 us)
Async XLA Ops:
  7.2 227.9 %copy-start = (f32[256,2048]{1,0:T(8,128)S(1)}, f32[256,2048]{1,0:T(8,128)}, u32[]{:S(2)}) copy-start(f32[256,2048]{1,0:T(8,128)} %param.15) | copy-start | bytes 6291460
  7.2 77.6 %all-gather.12.cloned.1.call-start = ((), (), s32[]{:S(2)}) async-start(), calls=%async_computation.6 | async-start | bytes 14155776 | tf_op jit(solution)/shard_map/all_gather | solution.py:27
  7.9 159.4 %reduce-scatter.2.cloned.1.call-start = ((), (), s32[]{:S(2)}) async-start(), calls=%async_computation.1 | async-start | bytes 2359296 | tf_op jit(solution)/shard_map/reduce_scatter | solution.py:29
  84.8 27.2 %copy-start.2 = (f32[3,2048,512]{2,1,0:T(8,128)S(1)}, f32[3,2048,512]{2,1,0:T(8,128)}, u32[]{:S(2)}) copy-start(f32[3,2048,512]{2,1,0:T(8,128)} %mul.26) | copy-start | bytes 37748740
  110.8 1.1 copy-start.3
  112.0 93.1 %copy-start.6 = (f32[256,256]{1,0:T(8,128)S(1)}, f32[256,256]{1,0:T(8,128)}, u32[]{:S(2)}) copy-start(f32[256,256]{1,0:T(8,128)} %param.9) | copy-start | bytes 786436
  125.9 79.2 %all-reduce.2.cloned.1.call-start = ((), (), s32[]{:S(2)}) async-start(), calls=%async_computation.2 | async-start | bytes 524288 | tf_op jit(solution)/shard_map/psum | solution.py:35
  167.3 67.7 %all-gather.6.cloned.1.call-start = ((), (), s32[]{:S(2)}) async-start(), calls=%async_computation.3 | async-start | bytes 2359296 | tf_op jit(solution)/shard_map/all_gather | solution.py:40
  206.8 62.4 %all-gather.8.cloned.1.call-start = ((), (), s32[]{:S(2)}) async-start(), calls=%async_computation.4 | async-start | bytes 2359296 | tf_op jit(solution)/shard_map/all_gather | solution.py:49
  240.9 117.0 %all-gather.10.cloned.1.call-start = ((), (), s32[]{:S(2)}) async-start(), calls=%async_computation.5 | async-start | bytes 14155776 | tf_op jit(solution)/shard_map/all_gather | solution.py:53
  246.3 22.9 %copy-start.4 = (f32[3,512,256]{2,1,0:T(8,128)S(1)}, f32[3,512,256]{2,1,0:T(8,128)}, u32[]{:S(2)}) copy-start(f32[3,512,256]{2,1,0:T(8,128)} %copy-done.3) | copy-start | bytes 4718596
  260.1 25.4 %copy-start.5 = (f32[256,256]{0,1:T(8,128)S(1)}, f32[256,256]{0,1:T(8,128)}, u32[]{:S(2)}) copy-start(f32[256,256]{0,1:T(8,128)} %convolution_bitcast_fusion) | copy-start | bytes 786436
  357.8 48.5 %copy-start.1 = (f32[256,2048]{1,0:T(8,128)S(1)}, f32[256,2048]{1,0:T(8,128)}, u32[]{:S(2)}) copy-start(f32[256,2048]{1,0:T(8,128)} %param.15) | copy-start | bytes 6291460
Sparse Core Ops, SparseCore 0:
  9.9 74.8 all-gather.11
  126.0 41.2 reduce-scatter.1
  169.8 35.2 all-reduce.1
  207.4 27.6 all-gather.5
  241.0 28.1 all-gather.7
  285.7 72.1 all-gather.9
where the time goes:
time: 414 us; the launch traced here: 413 us
  waiting for transfers between devices  243 us (59%)
  matrix products  107 us (26%)
  local copies, waits for them, and re-layouts  46 us (11%)
  between operations  14.2 us (3%)
    dot_general x2, matrix products, fold_stacked(): jnp.einsum('kij,kjr->kir', matrices, piece, precision=lax.Precision.HIGHEST)  71.5 us
    all_gather x1, waiting for transfers between devices, body(): lax.all_gather(residue, 'row', axis=1, tiled=True)  71.4 us
    all_gather x1, waiting for transfers between devices, body(): lax.all_gather(vectors, 'row', axis=1, tiled=True)  54.4 us
    reduce_scatter x1, waiting for transfers between devices, body(): lax.psum_scatter(jnp.einsum('kas,ksr->ar', lower_coupling, interim, preci...  41.3 us
    mul x4, local copies, waits for them, and re-layouts, masked_tiles(): return (shaped * weights).reshape(blocks, height, breadth)  40.8 us
    psum x1, waiting for transfers between devices, body(): layer_total = lax.psum(local_part, 'layer')  37.7 us
    all_gather x1, waiting for transfers between devices, body(): lax.all_gather(reduced, 'row', axis=0, tiled=True)  28 us
    dot_general x1, matrix products, body(): jnp.einsum('ksa,ar->ksr', columns, lax.all_gather(sol_root, 'row', axis=0...  16.3 us
  transfers between devices with their start and end apart: 6, of which 6 were waited for; matrix products, arithmetic and copies ran while one was open for 10% of the time, Pallas kernels for 0%

commit v1 on v0

v1 whole, which is shorter than its diff:
```python
import functools

import jax
import jax.numpy as jnp
from jax import lax
from jax.experimental import pallas as pl
from jax.experimental.pallas import tpu as pltpu
from jax.sharding import PartitionSpec as P

TILE = 128
CUBE = 8
MESH = pl.DeviceIdType.MESH
F32, BF16 = jnp.float32, jnp.bfloat16


def split(a):
    high = a.astype(BF16)
    return high, (a - high.astype(F32)).astype(BF16)


def dot3(a, b):
    ah, al = split(a)
    bh, bl = split(b)
    dot = functools.partial(jnp.dot, preferred_element_type=F32)
    return dot(ah, bh) + (dot(ah, bl) + dot(al, bh))


def gather_kernel(multiply, *refs):
    if multiply:
        x_ref, w_hbm, out_ref, held, weights, send_sem, recv_sem, w_sem = refs
    else:
        x_ref, out_ref, send_sem, recv_sem = refs
        held = out_ref
    count, depth, _ = x_ref.shape
    half = depth // 2
    me = lax.axis_index("row")
    layer = lax.axis_index("layer")
    core = lax.rem(me, 2)
    ax = lax.rem(me // 2, 2)
    ay = me // 4

    def place(fy, fx, fc):
        y = 1 - ay if fy else ay
        x = 1 - ax if fx else ax
        c = 1 - core if fc else core
        return y * 4 + x * 2 + c

    own, sib, xn, yn = place(0, 0, 0), place(0, 0, 1), place(0, 1, 0), place(1, 0, 0)
    diag, sx, sy, sd = place(1, 1, 0), place(0, 1, 1), place(1, 0, 1), place(1, 1, 1)

    barrier = pltpu.get_barrier_semaphore()
    for to in (sib, xn, yn):
        pl.semaphore_signal(barrier, inc=1, device_id=(layer, to), device_id_type=MESH)

    def weight_copy(k):
        return pltpu.make_async_copy(w_hbm.at[k], weights.at[k], w_sem.at[k])

    if multiply:
        for k in range(count):
            weight_copy(k).start()
    for k in range(count):
        held[k, own] = x_ref[k]
    pl.semaphore_wait(barrier, 3)

    low, high = pl.ds(0, half), pl.ds(half, half)
    routes = (
        (own, None, sib),
        (own, None, xn),
        (own, None, yn),
        (xn, low, yn),
        (xn, None, sib),
        (yn, high, xn),
        (yn, None, sib),
        (diag, low, sib),
        (diag, high, sib),
    )

    def route(slot, k):
        block, rows, to = routes[slot]
        ref = held.at[k, block] if rows is None else held.at[k, block, rows]
        return pltpu.make_async_remote_copy(
            src_ref=ref,
            dst_ref=ref,
            send_sem=send_sem.at[slot, k],
            recv_sem=recv_sem.at[slot, k],
            device_id=(layer, to),
            device_id_type=MESH,
        )

    def meet(k, block):
        if multiply:
            columns = pl.ds(pl.multiple_of(block * depth, depth), depth)
            out_ref[k] += dot3(weights[k, :, columns], held[k, block])

    for k in range(count):
        for slot in (1, 2, 0):
            route(slot, k).start()

    def first(k, carry):
        if multiply:
            weight_copy(k).wait()
            out_ref[k] = jnp.zeros(out_ref.shape[1:], F32)
            meet(k, own)
        return carry

    def second(k, carry):
        route(1, k).wait_recv()
        route(3, k).start()
        route(4, k).start()
        route(2, k).wait_recv()
        route(5, k).start()
        route(6, k).start()
        meet(k, xn)
        meet(k, yn)
        route(0, k).wait_recv()
        meet(k, sib)
        return carry

    def third(k, carry):
        route(3, k).wait_recv()
        route(7, k).start()
        route(5, k).wait_recv()
        route(8, k).start()
        route(4, k).wait_recv()
        meet(k, sx)
        route(6, k).wait_recv()
        meet(k, sy)
        meet(k, diag)
        route(7, k).wait_recv()
        route(8, k).wait_recv()
        meet(k, sd)
        return carry

    def last(k, carry):
        for slot in range(9):
            route(slot, k).wait_send()
        return carry

    for stage in (first, second, third, last):
        lax.fori_loop(0, count, stage, 0)


def gather_multiply(matrices, piece, collective_id):
    count, rows, wide = matrices.shape
    _, depth, breadth = piece.shape
    return pl.pallas_call(
        functools.partial(gather_kernel, True),
        out_shape=jax.ShapeDtypeStruct((count, rows, breadth), F32),
        in_specs=[pl.BlockSpec(memory_space=pltpu.VMEM), pl.BlockSpec(memory_space=pl.ANY)],
        out_specs=pl.BlockSpec(memory_space=pltpu.VMEM),
        scratch_shapes=[
            pltpu.VMEM((count, CUBE, depth, breadth), F32),
            pltpu.VMEM((count, rows, wide), F32),
            pltpu.SemaphoreType.DMA((9, count)),
            pltpu.SemaphoreType.DMA((9, count)),
            pltpu.SemaphoreType.DMA((count,)),
        ],
        compiler_params=pltpu.CompilerParams(
            collective_id=collective_id, has_side_effects=True, vmem_limit_bytes=56 << 20
        ),
        cost_estimate=pl.CostEstimate(
            flops=6 * count * rows * wide * breadth, bytes_accessed=4 * matrices.size, transcendentals=0
        ),
    )(piece, matrices)


def gather_only(piece, collective_id):
    depth, breadth = piece.shape
    out = pl.pallas_call(
        functools.partial(gather_kernel, False),
        out_shape=jax.ShapeDtypeStruct((1, CUBE, depth, breadth), F32),
        in_specs=[pl.BlockSpec(memory_space=pltpu.VMEM)],
        out_specs=pl.BlockSpec(memory_space=pltpu.VMEM),
        scratch_shapes=[pltpu.SemaphoreType.DMA((9, 1)), pltpu.SemaphoreType.DMA((9, 1))],
        compiler_params=pltpu.CompilerParams(
            collective_id=collective_id, has_side_effects=True, vmem_limit_bytes=16 << 20
        ),
    )(piece[None])
    return out.reshape(CUBE * depth, breadth)


def low_kernel(c_ref, m_ref, x_ref, o_ref):
    k = pl.program_id(1)

    @pl.when(k == 0)
    def _():
        o_ref[...] = jnp.zeros_like(o_ref)

    for t in range(c_ref.shape[1] // TILE):
        rows = pl.ds(t * TILE, TILE)
        o_ref[rows, :] += dot3(c_ref[0, rows, :] * m_ref[0, t], x_ref[k])


def masked_low(coupling, pattern, interim):
    count, height, wide = coupling.shape
    breadth = interim.shape[2]
    block = min(512, height)
    weights = jnp.repeat(pattern.astype(F32), TILE, axis=2)[:, :, None, :]
    return pl.pallas_call(
        low_kernel,
        grid=(height // block, count),
        out_shape=jax.ShapeDtypeStruct((height, breadth), F32),
        in_specs=[
            pl.BlockSpec((1, block, wide), lambda i, k: (k, i, 0)),
            pl.BlockSpec((1, block // TILE, 1, wide), lambda i, k: (k, i, 0, 0)),
            pl.BlockSpec(interim.shape, lambda i, k: (0, 0, 0)),
        ],
        out_specs=pl.BlockSpec((block, breadth), lambda i, k: (i, 0)),
        compiler_params=pltpu.CompilerParams(vmem_limit_bytes=32 << 20),
    )(coupling, weights, interim)


def up_kernel(u_ref, m_ref, s_ref, i_ref, o_ref):
    for t in range(u_ref.shape[1] // TILE):
        rows = pl.ds(t * TILE, TILE)
        o_ref[0, rows, :] = i_ref[0, rows, :] - dot3(u_ref[0, rows, :] * m_ref[0, t], s_ref[...])


def masked_up(coupling, pattern, sol_root, interim):
    count, height, wide = coupling.shape
    breadth = sol_root.shape[1]
    block = min(256, height)
    weights = jnp.repeat(jnp.transpose(pattern, (0, 2, 1)).astype(F32), TILE, axis=2)[:, :, None, :]
    return pl.pallas_call(
        up_kernel,
        grid=(count, height // block),
        out_shape=jax.ShapeDtypeStruct((count, height, breadth), F32),
        in_specs=[
            pl.BlockSpec((1, block, wide), lambda k, i: (k, i, 0)),
            pl.BlockSpec((1, block // TILE, 1, wide), lambda k, i: (k, i, 0, 0)),
            pl.BlockSpec(sol_root.shape, lambda k, i: (0, 0)),
            pl.BlockSpec((1, block, breadth), lambda k, i: (k, i, 0)),
        ],
        out_specs=pl.BlockSpec((1, block, breadth), lambda k, i: (k, i, 0)),
        compiler_params=pltpu.CompilerParams(vmem_limit_bytes=32 << 20),
    )(coupling, weights, sol_root, interim)


def fold(cube, matrices, piece, collective_id):
    if cube:
        return gather_multiply(matrices, piece, collective_id)
    whole = lax.all_gather(piece, "row", axis=1, tiled=True)
    return jnp.einsum("kij,kjr->kir", matrices, whole, precision=lax.Precision.HIGHEST)


def body(cube, rhs_sub, rhs_root, lower_inv, upper_inv, coupling_low, coupling_up, tile_mask, root_inv):
    pattern = tile_mask[0]
    interim = fold(cube, lower_inv[0], rhs_sub[0], 1)
    partial = masked_low(coupling_low[0], pattern, interim)
    partial = lax.psum_scatter(partial, "row", scatter_dimension=0, tiled=True)
    reduced = rhs_root - lax.psum(partial, "layer")
    sol_root = fold(cube, root_inv[None], reduced[None], 2)[0]
    if cube:
        whole = gather_only(sol_root, 3)
    else:
        whole = lax.all_gather(sol_root, "row", axis=0, tiled=True)
    residue = masked_up(coupling_up[0], pattern, whole, interim)
    solved = fold(cube, upper_inv[0], residue, 4)
    return solved[None], sol_root


def solution(mesh):
    return jax.shard_map(
        functools.partial(body, mesh.shape["row"] == CUBE),
        mesh=mesh,
        in_specs=(
            P("layer", None, "row", None),
            P("row", None),
            P("layer", None, "row", None),
            P("layer", None, "row", None),
            P("layer", None, None, "row"),
            P("layer", None, "row", None),
            P("layer", None, None, "row"),
            P("row", None),
        ),
        out_specs=(P("layer", None, "row", None), P("row", None)),
        check_vma=False,
    )
```

time: 414 us -> 279 us (0.67)
  Pallas kernels: 0 us -> 166 us
  waiting for transfers between devices: 243 us -> 79.2 us
  matrix products: 107 us -> 0 us
  local copies, waits for them, and re-layouts: 46 us -> 16.3 us
    pallas_call x0 -> x6, Pallas kernels: none -> 166 us  [the longest x3 137 us: gather_multiply(): pl.pallas_call(functools.partial(gather_kernel, True), out_shape=jax.Shap...]
    all_gather x4 -> x0, waiting for transfers between devices: 163 us -> none  [the longest x1 71.4 us: body(): lax.all_gather(residue, 'row', axis=1, tiled=True)]
    dot_general x5 -> x0, matrix products: 107 us -> none  [the longest x2 71.5 us: fold_stacked(): jnp.einsum('kij,kjr->kir', matrices, piece, precision=lax.Precision.HIGHEST)]
    mul x4 -> x0, local copies, waits for them, and re-layouts: 40.8 us -> none  [masked_tiles(): return (shaped * weights).reshape(blocks, height, breadth)]
    unnamed x16 -> x18, local copies, waits for them, and re-layouts: 5.03 us -> 16 us
  transfers between devices with their start and end apart: 6 -> 2, of which waited for: 6 -> 2; matrix products, arithmetic and copies ran while one was open for 10% -> 0% of each run, Pallas kernels for 0% -> 0%
where the time goes in v1:
time: 279 us; the launch traced here: 278 us
  Pallas kernels  166 us (59%)
  waiting for transfers between devices  79.2 us (28%)
  local copies, waits for them, and re-layouts  16.3 us (6%)
  between operations  14.1 us (5%)
    pallas_call x3, Pallas kernels, gather_multiply(): pl.pallas_call(functools.partial(gather_kernel, True), out_shape=jax.Shap...  137 us
    reduce_scatter x1, waiting for transfers between devices, body(): partial = lax.psum_scatter(partial, 'row', scatter_dimension=0, tiled=True)  41.4 us
    psum x1, waiting for transfers between devices, body(): reduced = rhs_root - lax.psum(partial, 'layer')  37.8 us
    unnamed x18, local copies, waits for them, and re-layouts  16 us
    pallas_call x1, Pallas kernels, gather_only(): pl.pallas_call(functools.partial(gather_kernel, False), out_shape=jax.Sha...  14.2 us
    pallas_call x1, Pallas kernels, masked_low(): pl.pallas_call(low_kernel, grid=(height // block, count), out_shape=jax.S...  8.75 us
    pallas_call x1, Pallas kernels, masked_up(): pl.pallas_call(up_kernel, grid=(count, height // block), out_shape=jax.Sh...  6.37 us
  transfers between devices with their start and end apart: 2, of which 2 were waited for; matrix products, arithmetic and copies ran while one was open for 0% of the time, Pallas kernels for 0%

profile of v1, /device:TPU:0, one launch (start us, length us, event | category | flops | bytes accessed | tf_op | source)
XLA Modules:
  0.0 278.4 jit_solution(6642727643169244416)
XLA Ops:
  7.2 0.0 reduce-scatter.2.cloned.1.call-start
  7.2 0.7 convert_bitcast_fusion.1
  7.9 0.1 copy.10
  8.0 61.3 %shard_map.95.x_ref.i_ref = f32[3,512,256]{2,1,0:T(8,128)} custom-call(f32[3,512,256]{2,1,0:T(8,128)} %bitcast.28, f32[3,512,4096]{2,1,0:T(8,128)} %bitcast.25), custom_call_target="tpu_custom_call" | custom-call | flops 9663676416 | bytes 25165824 | tf_op jit(solution)/shard_map/pallas_call | solution.py:146
  69.3 0.1 broadcast_in_dim.16
  69.4 0.0 copy-start.1
  69.5 4.6 %copy-done.1 = f32[1,3,2048,512]{3,2,1,0:T(8,128)S(1)} copy-done((f32[1,3,2048,512]{3,2,1,0:T(8,128)S(1)}, f32[1,3,2048,512]{3,2,1,0:T(8,128)}, u32[]{:S(2)}) %copy-start.1) | copy-done | bytes 12582936
  74.0 1.4 copy-done.2
  75.4 8.7 %shard_map.96 = f32[2048,256]{1,0:T(8,128)} custom-call(f32[3,2048,512]{2,1,0:T(8,128)S(1)} %bitcast.19, f32[3,16,1,512]{3,2,1,0:T(1,128)S(1)} %bitcast.23, f32[3,512,256]{2,1,0:T(8,128)S(1)} %copy-done.2), custom_call_target="tpu_custom_call" | custom-call | tf_op jit(solution)/shard_map/pallas_call | solution.py:199
  84.2 0.0 reduce-scatter.2.cloned.1.call-update
  84.2 0.2 all-reduce.2.cloned.1.call-start
  84.4 41.4 %reduce-scatter.2.cloned.1.call-done = f32[256,256]{1,0:T(8,128)} async-done(((f32[2048,256]{1,0:T(8,128)}), f32[256,256]{1,0:T(8,128)}) %reduce-scatter.2.cloned.1.call-update) | async-done | bytes 262160 | tf_op jit(solution)/shard_map/reduce_scatter | solution.py:250
  125.8 0.0 all-reduce.2.cloned.1.call-update
  125.8 37.8 %all-reduce.2.cloned.1.call-done = f32[256,256]{1,0:T(8,128)} async-done(((f32[256,256]{1,0:T(8,128)}), f32[256,256]{1,0:T(8,128)}) %all-reduce.2.cloned.1.call-update) | async-done | bytes 262160 | tf_op jit(solution)/shard_map/psum | solution.py:251
  163.6 0.0 copy-done.7
  163.6 1.7 subtract_bitcast_fusion.refs_0_
  165.3 16.1 %shard_map.97.refs_0_ = f32[1,256,256]{2,1,0:T(8,128)} custom-call(f32[1,256,256]{2,1,0:T(8,128)} %subtract_bitcast_fusion.refs_0_, f32[1,256,2048]{2,1,0:T(8,128)} %bitcast.27), custom_call_target="tpu_custom_call" | custom-call | flops 805306368 | bytes 2097152 | tf_op jit(solution)/shard_map/pallas_call | solution.py:146
  181.4 0.0 copy-start.5
  181.4 0.9 copy-done.5
  182.3 14.2 %shard_map.98 = f32[1,8,256,256]{3,2,1,0:T(8,128)S(1)} custom-call(f32[1,256,256]{2,1,0:T(8,128)S(1)} %copy-done.5), custom_call_target="tpu_custom_call" | custom-call | tf_op jit(solution)/shard_map/pallas_call | solution.py:169
  196.6 0.1 broadcast_in_dim.15
  196.6 0.0 copy-done.3
  196.7 0.0 copy-start
  196.7 4.6 %copy-done = f32[1,3,512,2048]{3,2,1,0:T(8,128)S(1)} copy-done((f32[1,3,512,2048]{3,2,1,0:T(8,128)S(1)}, f32[1,3,512,2048]{3,2,1,0:T(8,128)}, u32[]{:S(2)}) %copy-start) | copy-done | bytes 12582936
  201.2 6.4 %shard_map.99.refs_0_ = f32[3,512,256]{2,1,0:T(8,128)S(1)} custom-call(f32[3,512,2048]{2,1,0:T(8,128)S(1)} %bitcast.18, f32[3,4,1,2048]{3,2,1,0:T(1,128)S(1)} %bitcast.22, f32[2048,256]{1,0:T(8,128)S(1)} %bitcast.20, f32[3,512,256]{2,1,0:T(8,128)S(1)} %copy-done.3), custom_call_target="tpu_custom_call" | custom-call | tf_op jit(solution)/shard_map/pallas_call | solution.py:224
  207.6 0.0 copy-start.4
  207.6 1.1 copy-done.4
  208.8 59.4 %shard_map.100 = f32[3,512,256]{2,1,0:T(8,128)} custom-call(f32[3,512,256]{2,1,0:T(8,128)} %copy-done.4, f32[3,512,4096]{2,1,0:T(8,128)} %bitcast.26), custom_call_target="tpu_custom_call" | custom-call | flops 9663676416 | bytes 25165824 | tf_op jit(solution)/shard_map/pallas_call | solution.py:146
  268.2 0.0 copy-start.6
  268.2 2.7 copy.14
  270.9 0.0 copy-done.6
  270.9 0.7 copy.15
  (3 shorter events, 0.0 us)
Async XLA Ops:
  7.2 118.7 %reduce-scatter.2.cloned.1.call-start = ((), (), s32[]{:S(2)}) async-start(), calls=%async_computation.1 | async-start | bytes 2359296 | tf_op jit(solution)/shard_map/reduce_scatter | solution.py:250
  69.4 4.6 %copy-start.1 = (f32[1,3,2048,512]{3,2,1,0:T(8,128)S(1)}, f32[1,3,2048,512]{3,2,1,0:T(8,128)}, u32[]{:S(2)}) copy-start(f32[1,3,2048,512]{3,2,1,0:T(8,128)} %param.12) | copy-start | bytes 37748740
  74.0 1.4 copy-start.2
  84.2 79.4 %copy-start.7 = (f32[256,256]{1,0:T(8,128)S(1)}, f32[256,256]{1,0:T(8,128)}, u32[]{:S(2)}) copy-start(f32[256,256]{1,0:T(8,128)} %param.9) | copy-start | bytes 786436
  84.2 79.4 %all-reduce.2.cloned.1.call-start = ((), (), s32[]{:S(2)}) async-start(), calls=%async_computation.2 | async-start | bytes 524288 | tf_op jit(solution)/shard_map/psum | solution.py:251
  165.3 31.3 %copy-start.3 = (f32[3,512,256]{2,1,0:T(8,128)S(1)}, f32[3,512,256]{2,1,0:T(8,128)}, u32[]{:S(2)}) copy-start(f32[3,512,256]{2,1,0:T(8,128)} %shard_map.95.x_ref.i_ref) | copy-start | bytes 4718596
  181.4 1.0 copy-start.5
  196.7 4.6 %copy-start = (f32[1,3,512,2048]{3,2,1,0:T(8,128)S(1)}, f32[1,3,512,2048]{3,2,1,0:T(8,128)}, u32[]{:S(2)}) copy-start(f32[1,3,512,2048]{3,2,1,0:T(8,128)} %param.13) | copy-start | bytes 37748740
  207.6 1.1 copy-start.4
  268.2 2.7 copy-start.6
Sparse Core Ops, SparseCore 0:
  84.3 41.4 reduce-scatter.1
  128.3 35.2 all-reduce.1
